TPU v7x, 32 devices: a whole 2x2x4 slice. The times are simulated.
32 devices in a mesh: dev: 32 (over z, y, x, core).
Axes of the slice: x: 2, y: 2, z: 4, core: 2. Of those that a mesh axis runs over, the one named last changes fastest.
Arguments:
- vectors: bfloat16 [8, 524288], P(None, 'dev'), may hold values from -1.5 to 1.5
- points: float32 [3, 524288], P(None, 'dev'), may hold values from -4 to 4
- leaf_basis: bfloat16 [2048, 64, 256], P('dev'), may hold values from -0.375 to 0.375
- near_list: int32 [2048, 8], P('dev'), may hold values from -32 to 32, as said below
- far_list: int32 [1984, 4], P('dev'), may hold values from -32 to 32, as said below
- transfer: bfloat16 [2016, 64, 128], P('dev'), may hold values from -0.625 to 0.625
- skeleton: float32 [2016, 192], P('dev'), may hold values from -4 to 4
- transfer_top: bfloat16 [31, 64, 128], replicated, may hold values from -0.625 to 0.625
- skeleton_top: float32 [30, 192], replicated, may hold values from -4 to 4
Outputs:
- product: float32 [8, 524288], P(None, 'dev')
Inputs may be any that keep to these rules, and one draw needn't show every extreme that they name: `near_list`: slot 0 of every row holds 0 (the leaf itself); every other slot holds 0 (empty) or a nonzero offset such that the leaf plus the offset is a leaf; the nonzero offsets of a row are distinct. `far_list`: rows follow the numbering of the transfer rows of levels 1 to log2(64) - 1. An entry is 0 (empty) or a nonzero offset of magnitude 2 or more and at most that level's clusters on one device, such that the cluster plus the offset is a cluster of the same level; the nonzero offsets of a row are distinct.
All inputs are finite; a program needn't handle non-finite values.
Results may differ from a plain program's by a relative error of at most 0.002.
Values may be sent and summed in bfloat16 or wider, within the bound.
A program may use at most 64 MiB of HBM per device.

v0:
```python
import math

import jax
import jax.numpy as jnp
from jax import lax
from jax.experimental import pallas as pl
from jax.experimental.pallas import tpu as pltpu
from jax.sharding import PartitionSpec as P

F32 = jnp.float32
BF16 = jnp.bfloat16
LOG2E = math.log2(math.e)
TINY = 1e-30
FEATURES = 48
GROUP = 8
STRIP = 64
MESH = pl.DeviceIdType.MESH
VMEM_BYTES = 56 * 1024 * 1024


def loop(count, unroll, step):
    unroll = min(unroll, count)

    def several(index, carry):
        for part in range(unroll):
            step(index * unroll + part)
        return carry

    lax.fori_loop(0, count // unroll, several, 0)


def level_row(leaf_count, level):
    return leaf_count - (leaf_count >> (level - 1))


def three_pieces(values):
    first = values.astype(BF16).astype(F32)
    rest = values - first
    second = rest.astype(BF16).astype(F32)
    return first, second, rest - second


def distance_factors(cells):
    row = lax.broadcasted_iota(jnp.int32, cells.shape, 0)
    scaled = jnp.where(row < 3, cells * LOG2E, 0.0)
    norms = jnp.sum(scaled * scaled, axis=0, keepdims=True)
    source = jnp.where(row == 3, norms, jnp.where(row == 4, 1.0, scaled))
    target = jnp.where(row == 3, 1.0, jnp.where(row == 4, norms, -2.0 * scaled))
    s1, s2, s3 = three_pieces(source)
    t1, t2, t3 = three_pieces(target)
    sources = jnp.concatenate([s1, s1, s2, s2, s1, s3], axis=0).astype(BF16)
    targets = jnp.concatenate([t1, t2, t1, t2, t3, t1], axis=0).astype(BF16)
    return sources, targets


def decay(squares):
    kept = jnp.maximum(squares, TINY)
    return jnp.exp2(-(kept * lax.rsqrt(kept)))


def product_rows(left, right):
    return lax.dot_general(left, right, (((0,), (0,)), ((), ())), preferred_element_type=F32)


def product(left, right):
    return lax.dot_general(left, right, (((1,), (0,)), ((), ())), preferred_element_type=F32)


def product_across(left, right):
    return lax.dot_general(left, right, (((1,), (1,)), ((), ())), preferred_element_type=F32)


def two_pieces(values):
    first = values.astype(BF16).astype(F32)
    return jnp.concatenate([first, values - first], axis=0).astype(BF16)


def fold(values):
    half = values.shape[0] // 2
    return values[:half] + values[half:]


def skeleton_cells(row):
    rank = row.shape[1] // 3
    parts = [row[:, c * rank : (c + 1) * rank] for c in range(3)]
    return jnp.concatenate(parts + [jnp.zeros((5, rank), F32)], axis=0)


def task_cells(offsets, rank):
    slots, leaf_dev = offsets.shape
    slot = lax.broadcasted_iota(jnp.int32, offsets.shape, 0)
    spot = lax.broadcasted_iota(jnp.int32, offsets.shape, 1)
    used = jnp.where((slot == 0) | (offsets != 0), 1.0, 0.0)
    lower = jnp.sum(jnp.where(spot < leaf_dev // 2, used, 0.0), keepdims=True)
    upper = jnp.sum(jnp.where(spot < leaf_dev // 2, 0.0, used), keepdims=True)
    row = lax.broadcasted_iota(jnp.int32, (8, rank), 0)
    column = lax.broadcasted_iota(jnp.int32, (8, rank), 1)
    counts = jnp.where(column == 0, lower, jnp.where(column == 1, upper, 0.0))
    return jnp.where(row == 5, counts, 0.0)


def up_kernel(
    list_ref,
    points_ref,
    vec_ref,
    basis_ref,
    transfer_ref,
    skeleton_ref,
    table_ref,
    table_left_ref,
    table_right_ref,
    roots_ref,
    points_left_ref,
    points_right_ref,
    vec_left_ref,
    vec_right_ref,
    list_left_ref,
    list_right_ref,
    pair_ref,
    send_sem,
    recv_sem,
    root_send_sem,
    root_recv_sem,
    own_sem,
):
    leaf_dev, rank, leaf = basis_ref.shape
    local = leaf_dev.bit_length() - 1
    rows = leaf_dev - 1
    devices = roots_ref.shape[0]
    me = lax.axis_index("dev")
    right = (me + 1) % devices
    left = (me + devices - 1) % devices
    has_right = me < devices - 1
    has_left = me > 0

    barrier = pltpu.get_barrier_semaphore()

    def greet(shift, carry):
        pl.semaphore_signal(
            barrier, inc=1, device_id=((me + shift) % devices,), device_id_type=MESH
        )
        return carry

    lax.fori_loop(1, devices, greet, 0)
    pl.semaphore_wait(barrier, devices - 1)

    def beside(source, arrival, device, index):
        return pltpu.make_async_remote_copy(
            src_ref=source,
            dst_ref=arrival,
            send_sem=send_sem.at[index],
            recv_sem=recv_sem.at[index],
            device_id=(device,),
            device_id_type=MESH,
        )

    leaf_right = [
        beside(points_ref, points_left_ref, right, 0),
        beside(vec_ref, vec_left_ref, right, 1),
        beside(list_ref, list_left_ref, right, 2),
    ]
    leaf_left = [
        beside(points_ref, points_right_ref, left, 3),
        beside(vec_ref, vec_right_ref, left, 4),
        beside(list_ref, list_right_ref, left, 5),
    ]
    table_right = beside(table_ref, table_left_ref, right, 6)
    table_left = beside(table_ref, table_right_ref, left, 7)

    @pl.when(has_right)
    def _():
        for copy in leaf_right:
            copy.start()

    @pl.when(has_left)
    def _():
        for copy in leaf_left:
            copy.start()

    def leaf_pair(pair):
        halves = []
        for part in range(2):
            spot = pair * 2 + part
            own = vec_ref[:, pl.ds(pl.multiple_of(spot * leaf, leaf), leaf)]
            halves.append(product_across(own, basis_ref[spot]))
        pair_ref[pair] = jnp.concatenate(halves, axis=1)

    loop(leaf_dev // 2, 8, leaf_pair)
    joined = [pair_ref[pair] for pair in range(leaf_dev // 2)]
    for level in range(1, local + 1):
        first = level_row(leaf_dev, level)
        coefs = []
        for spot in range(leaf_dev >> level):
            coef = fold(product_across(two_pieces(joined[spot]), transfer_ref[first + spot]))
            cells = skeleton_cells(skeleton_ref[pl.ds(first + spot, 1), :])
            if level == local:
                cells = cells + task_cells(list_ref[...], rank)
            table_ref[first + spot] = jnp.concatenate([coef, cells], axis=1)
            coefs.append(coef)
        joined = [
            jnp.concatenate(coefs[2 * spot : 2 * spot + 2], axis=1)
            for spot in range(len(coefs) // 2)
        ]

    root = table_ref.at[pl.ds(rows - 1, 1)]
    mine = roots_ref.at[pl.ds(me, 1)]

    def root_copy(shift):
        return pltpu.make_async_remote_copy(
            src_ref=root,
            dst_ref=mine,
            send_sem=root_send_sem.at[shift],
            recv_sem=root_recv_sem.at[shift],
            device_id=((me + shift) % devices,),
            device_id_type=MESH,
        )

    def send_root(shift, carry):
        root_copy(shift).start()
        return carry

    def wait_root(shift, carry):
        root_copy(shift).wait()
        return carry

    @pl.when(has_right)
    def _():
        table_right.start()

    @pl.when(has_left)
    def _():
        table_left.start()

    lax.fori_loop(1, devices, send_root, 0)
    own_copy = pltpu.make_async_copy(root, mine, own_sem)
    own_copy.start()

    @pl.when(has_right)
    def _():
        for copy in leaf_right + [table_right]:
            copy.wait_send()
        for copy in leaf_left + [table_left]:
            copy.wait_recv()

    @pl.when(has_left)
    def _():
        for copy in leaf_left + [table_left]:
            copy.wait_send()
        for copy in leaf_right + [table_right]:
            copy.wait_recv()

    lax.fori_loop(1, devices, wait_root, 0)
    own_copy.wait()


def balance(counts_ref, me):
    devices = counts_ref.shape[0]

    def total_and_most(spot, carry):
        total, most = carry
        own = counts_ref[spot, 0] + counts_ref[spot, 1]
        return total + own, jnp.maximum(most, own)

    total, most = lax.fori_loop(0, devices, total_and_most, (0, 0))

    def hand(spot, flow, limit):
        own = counts_ref[spot, 0] + counts_ref[spot, 1]
        after = jnp.minimum(spot + 1, devices - 1)
        lower = jnp.where(spot + 1 < devices, counts_ref[after, 0], 0)
        upper = jnp.where(spot + 1 < devices, counts_ref[spot, 1], 0)
        flow = jnp.maximum(own + flow - limit, -lower)
        return flow, jnp.where(flow <= upper, 1, 0)

    def halve(step, carry):
        low, high = carry
        limit = (low + high) >> 1

        def walk(spot, state):
            flow, fits = state
            flow, here = hand(spot, flow, limit)
            return flow, fits & here

        _, fits = lax.fori_loop(0, devices, walk, (0, 1))
        return jnp.where(fits == 1, low, limit + 1), jnp.where(fits == 1, limit, high)

    _, limit = lax.fori_loop(0, 6, halve, (total >> (devices.bit_length() - 1), most))
    before = lax.fori_loop(0, me, lambda spot, flow: hand(spot, flow, limit)[0], 0)
    return before, hand(me, before, limit)[0]


def near_kernel(
    counts_ref,
    list_ref,
    list_left_ref,
    list_right_ref,
    points_ref,
    points_left_ref,
    points_right_ref,
    vec_ref,
    vec_left_ref,
    vec_right_ref,
    out_ref,
    source_ref,
    target_ref,
    wide_vec_ref,
    task_target_ref,
    task_source_ref,
):
    slots, leaf_dev = list_ref.shape
    leaf = points_ref.shape[1] // leaf_dev
    half = leaf_dev // 2
    cells = leaf_dev * leaf
    edge = half * leaf
    wide = 3 * leaf_dev
    chunk = 4 * leaf
    me = lax.axis_index("dev")

    def fill(points, vecs, base, first, length, aimed):
        def step(index):
            start = pl.multiple_of(first + index * chunk, chunk)
            spot = pl.multiple_of(base + start, chunk)
            part = points[:, pl.ds(start, chunk)]
            part = jnp.concatenate([part, jnp.zeros((5, chunk), F32)], axis=0)
            sources, targets = distance_factors(part)
            source_ref[:, pl.ds(spot, chunk)] = sources
            if aimed:
                aim = pl.ds(pl.multiple_of(spot - edge, chunk), chunk)
                target_ref[:, aim] = targets
                out_ref[:, aim] = jnp.zeros((out_ref.shape[0], chunk), F32)
            wide_vec_ref[:, pl.ds(spot, chunk)] = vecs[:, pl.ds(start, chunk)].astype(F32)

        loop(length // chunk, 2, step)

    fill(points_left_ref, vec_left_ref, 0, 0, edge, False)
    fill(points_left_ref, vec_left_ref, 0, edge, edge, True)
    fill(points_ref, vec_ref, cells, 0, cells, True)
    fill(points_right_ref, vec_right_ref, 2 * cells, 0, edge, True)
    fill(points_right_ref, vec_right_ref, 2 * cells, edge, edge, False)
    empty = pl.ds(wide * leaf, leaf)
    source_ref[:, empty] = jnp.zeros((FEATURES, leaf), BF16)
    wide_vec_ref[:, empty] = jnp.zeros((wide_vec_ref.shape[0], leaf), F32)

    before, after = balance(counts_ref, me)

    def enlist(lists, base, first, last, low, high, count):
        def step(spot, carry):
            order, count = carry
            for slot in range(slots):
                offset = lists[slot, spot]
                task_target_ref[count] = base + spot - half
                task_source_ref[count] = base + spot + offset
                used = 1 if slot == 0 else jnp.where(offset != 0, 1, 0)
                kept = jnp.where((order >= low) & (order < high), used, 0)
                order = order + used
                count = count + kept
            return order, count

        return lax.fori_loop(first, last, step, (0, count))[1]

    before_upper = counts_ref[jnp.maximum(me - 1, 0), 1]
    own_tasks = counts_ref[me, 0] + counts_ref[me, 1]
    count = enlist(
        list_ref,
        leaf_dev,
        0,
        leaf_dev,
        jnp.maximum(-before, 0),
        own_tasks - jnp.maximum(after, 0),
        0,
    )
    count = enlist(
        list_left_ref,
        0,
        jnp.where(before > 0, half, leaf_dev),
        leaf_dev,
        before_upper - before,
        before_upper,
        count,
    )
    count = enlist(
        list_right_ref, 2 * leaf_dev, 0, jnp.where(after < 0, half, 0), 0, -after, count
    )
    for extra in range(GROUP):
        task_target_ref[count + extra] = 0
        task_source_ref[count + extra] = wide

    def several(index, carry):
        targets, vecs, factors = [], [], []
        for part in range(GROUP):
            target = pl.multiple_of(task_target_ref[index * GROUP + part] * leaf, leaf)
            source = pl.multiple_of(task_source_ref[index * GROUP + part] * leaf, leaf)
            targets.append(target)
            vecs.append(wide_vec_ref[:, pl.ds(source, leaf)].astype(BF16))
            factors.append((source_ref[:, pl.ds(source, leaf)], target_ref[:, pl.ds(target, leaf)]))
        strips = [(part, start) for part in range(GROUP) for start in range(0, leaf, STRIP)]
        tiles = [[] for _ in range(GROUP)]
        results = []
        ahead, standing = None, None
        for strip in strips + [None]:
            waiting, ahead = ahead, None
            if strip is not None:
                part, start = strip
                if start == 0:
                    standing = factors[part][0].T
                ahead = part, product(standing[start : start + STRIP], factors[part][1])
            if waiting is not None:
                part, squares = waiting
                tiles[part].append(decay(squares).astype(BF16))
                if len(tiles[part]) == leaf // STRIP:
                    results.append(product(vecs[part], jnp.concatenate(tiles[part], axis=0)))
        for target, result in zip(targets, results):
            out_ref[:, pl.ds(target, leaf)] += result
        return carry

    lax.fori_loop(0, (count + GROUP - 1) // GROUP, several, 0)


def couple(cells, rows, weights):
    rank = cells.shape[1]
    coefs = jnp.concatenate(
        [row[:, :rank] * weight for row, weight in zip(rows, weights)], axis=1
    )
    partner_cells = jnp.concatenate([row[:, rank:] for row in rows], axis=1)
    sources, _ = distance_factors(partner_cells)
    _, targets = distance_factors(cells)
    tile = decay(product_rows(sources, targets))
    main = tile.astype(BF16)
    rest = (tile - main.astype(F32)).astype(BF16)
    pieces = two_pieces(coefs)
    return fold(product(pieces, main) + product(pieces, rest))


def down_kernel(
    far_ref,
    near_ref,
    basis_ref,
    transfer_ref,
    own_ref,
    left_ref,
    right_ref,
    roots_ref,
    transfer_top_ref,
    skeleton_top_ref,
    out_ref,
    wide_ref,
    top_ref,
    coupled_ref,
    field_ref,
    help_ref,
    send_sem,
    recv_sem,
):
    leaf_dev, rank, leaf = basis_ref.shape
    devices = roots_ref.shape[0]
    local = leaf_dev.bit_length() - 1
    top = devices.bit_length() - 1
    rows = leaf_dev - 1
    me = lax.axis_index("dev")
    half = leaf_dev // 2
    edge = half * leaf
    has_right = me < devices - 1
    has_left = me > 0
    right = (me + 1) % devices
    left = (me + devices - 1) % devices

    barrier = pltpu.get_barrier_semaphore()

    @pl.when(has_right)
    def _():
        pl.semaphore_signal(barrier, inc=1, device_id=(right,), device_id_type=MESH)

    @pl.when(has_left)
    def _():
        pl.semaphore_signal(barrier, inc=1, device_id=(left,), device_id_type=MESH)

    pl.semaphore_wait(barrier, jnp.where(has_right, 1, 0) + jnp.where(has_left, 1, 0))

    def handed_back(start, index, device):
        return pltpu.make_async_remote_copy(
            src_ref=near_ref.at[:, pl.ds(start, edge)],
            dst_ref=help_ref.at[index],
            send_sem=send_sem.at[index],
            recv_sem=recv_sem.at[index],
            device_id=(device,),
            device_id_type=MESH,
        )

    to_right = handed_back(edge + leaf_dev * leaf, 0, right)
    to_left = handed_back(0, 1, left)

    @pl.when(has_right)
    def _():
        to_right.start()

    @pl.when(has_left)
    def _():
        to_left.start()

    for part, ref in enumerate((left_ref, own_ref, right_ref)):
        wide_ref[part * rows : (part + 1) * rows] = ref[...]
    top_ref[0:devices] = roots_ref[...]

    def top_row(step, spot):
        if step == 0:
            return spot
        return devices + devices - (devices >> (step - 1)) + spot

    for step in range(1, top):
        first = devices - (devices >> (step - 1))

        def lift(spot, step=step, first=first):
            joined = jnp.concatenate(
                [top_ref[top_row(step - 1, 2 * spot + part)][:, :rank] for part in range(2)],
                axis=1,
            )
            coef = fold(product_across(two_pieces(joined), transfer_top_ref[first + spot]))
            cells = skeleton_cells(skeleton_top_ref[pl.ds(first + spot, 1), :])
            top_ref[top_row(step, spot)] = jnp.concatenate([coef, cells], axis=1)

        loop(devices >> step, 16, lift)

    for level in range(1, local):
        first = level_row(leaf_dev, level)
        count = leaf_dev >> level

        def couple_pair(pair, first=first, count=count):
            halves = []
            for part in range(2):
                spot = pair * 2 + part
                partners, weights = [], []
                for slot in range(far_ref.shape[0]):
                    offset = far_ref[slot, first + spot]
                    partner = spot + offset
                    side = jnp.where(partner < 0, 0, jnp.where(partner < count, 1, 2))
                    partners.append(wide_ref[side * rows + first + partner - (side - 1) * count])
                    weights.append(jnp.where(offset != 0, 1.0, 0.0))
                mine = wide_ref[rows + first + spot]
                halves.append(couple(mine[:, rank:], partners, weights))
            coupled_ref[first // 2 + pair] = jnp.concatenate(halves, axis=1)

        loop(count // 2, 4, couple_pair)

    field = None
    for step in range(top - 1, -1, -1):
        spot = me >> step
        mine = top_ref[top_row(step, spot)]
        sibling = top_ref[top_row(step, spot ^ 1)]
        coupled = couple(mine[:, rank:], [sibling], [1.0])
        if field is None:
            field = coupled
        else:
            parent = devices - (devices >> step) + (spot >> 1)
            both = fold(product(two_pieces(field), transfer_top_ref[parent]))
            field = jnp.where((spot & 1) == 1, both[:, rank:], both[:, :rank]) + coupled

    fields = [field]
    for level in range(local - 1, -1, -1):
        first = level_row(leaf_dev, level + 1)
        below = []
        for spot, parent in enumerate(fields):
            both = fold(product(two_pieces(parent), transfer_ref[first + spot]))
            if level >= 1:
                both = both + coupled_ref[level_row(leaf_dev, level) // 2 + spot]
                below += [both[:, :rank], both[:, rank:]]
            else:
                field_ref[spot] = both
        fields = below

    @pl.when(has_right)
    def _():
        to_right.wait_send()
        to_left.wait_recv()

    @pl.when(has_left)
    def _():
        to_left.wait_send()
        to_right.wait_recv()

    @pl.when(jnp.logical_not(has_left))
    def _():
        help_ref[0] = jnp.zeros((help_ref.shape[1], edge), F32)

    @pl.when(jnp.logical_not(has_right))
    def _():
        help_ref[1] = jnp.zeros((help_ref.shape[1], edge), F32)

    for side in range(2):

        def expand(pair, side=side):
            both = field_ref[side * (half // 2) + pair]
            for part in range(2):
                spot = pair * 2 + part
                pieces = two_pieces(both[:, part * rank : (part + 1) * rank])
                inner = pl.multiple_of(spot * leaf, leaf)
                here = pl.multiple_of(side * edge + spot * leaf, leaf)
                there = pl.multiple_of(edge + side * edge + spot * leaf, leaf)
                near = near_ref[:, pl.ds(there, leaf)] + help_ref[side, :, pl.ds(inner, leaf)]
                far = fold(product(pieces, basis_ref[side * half + spot]))
                out_ref[:, pl.ds(here, leaf)] = near + far

        loop(half // 2, 4, expand)


def body(
    vectors, points, leaf_basis, near_list, far_list, transfer, skeleton, transfer_top, skeleton_top
):
    rhs, cells = vectors.shape
    leaf_dev, rank, leaf = leaf_basis.shape
    slots = near_list.shape[1]
    devices = lax.axis_size("dev")
    wide = 3 * leaf_dev
    edge = cells // 2
    rows = leaf_dev - 1
    vmem = pl.BlockSpec(memory_space=pltpu.VMEM)
    smem = pl.BlockSpec(memory_space=pltpu.SMEM)
    hbm = pl.BlockSpec(memory_space=pl.ANY)
    params = pltpu.CompilerParams(vmem_limit_bytes=VMEM_BYTES)

    table_shape = jax.ShapeDtypeStruct((rows, rhs, 2 * rank), F32)
    points_shape = jax.ShapeDtypeStruct(points.shape, points.dtype)
    lists = near_list.T
    list_shape = jax.ShapeDtypeStruct(lists.shape, lists.dtype)
    vec_shape = jax.ShapeDtypeStruct(vectors.shape, vectors.dtype)
    (
        table,
        table_left,
        table_right,
        roots,
        points_left,
        points_right,
        vec_left,
        vec_right,
        list_left,
        list_right,
    ) = pl.pallas_call(
        up_kernel,
        out_shape=(
            table_shape,
            table_shape,
            table_shape,
            jax.ShapeDtypeStruct((devices, rhs, 2 * rank), F32),
            points_shape,
            points_shape,
            vec_shape,
            vec_shape,
            list_shape,
            list_shape,
        ),
        in_specs=[vmem] * 6,
        out_specs=(vmem,) + (hbm,) * 9,
        scratch_shapes=[
            pltpu.VMEM((leaf_dev // 2, rhs, 2 * rank), F32),
            pltpu.SemaphoreType.DMA((8,)),
            pltpu.SemaphoreType.DMA((8,)),
            pltpu.SemaphoreType.DMA((devices,)),
            pltpu.SemaphoreType.DMA((devices,)),
            pltpu.SemaphoreType.DMA,
        ],
        compiler_params=pltpu.CompilerParams(
            vmem_limit_bytes=VMEM_BYTES, collective_id=0, has_side_effects=True
        ),
        cost_estimate=pl.CostEstimate(
            flops=2 * 256 * 256 * 256 * 64, bytes_accessed=4 * 2**20, transcendentals=0
        ),
        name="upward",
    )(lists, points, vectors, leaf_basis, transfer, skeleton)
    counts = roots[:, 5, rank : rank + 2].astype(jnp.int32)

    tasks = 2 * leaf_dev * slots + 2 * GROUP
    near = pl.pallas_call(
        near_kernel,
        out_shape=jax.ShapeDtypeStruct((rhs, cells + 2 * edge), F32),
        in_specs=[smem] * 4 + [vmem] * 6,
        out_specs=vmem,
        scratch_shapes=[
            pltpu.VMEM((FEATURES, (wide + 1) * leaf), BF16),
            pltpu.VMEM((FEATURES, cells + 2 * edge), BF16),
            pltpu.VMEM((rhs, (wide + 1) * leaf), F32),
            pltpu.SMEM((tasks,), jnp.int32),
            pltpu.SMEM((tasks,), jnp.int32),
        ],
        compiler_params=params,
        cost_estimate=pl.CostEstimate(
            flops=2 * 256 * 256 * 256 * 64 * 20, bytes_accessed=2 * 2**20, transcendentals=2**25
        ),
        name="near",
    )(
        counts,
        lists,
        list_left,
        list_right,
        points,
        points_left,
        points_right,
        vectors,
        vec_left,
        vec_right,
    )

    return pl.pallas_call(
        down_kernel,
        out_shape=jax.ShapeDtypeStruct((rhs, cells), F32),
        in_specs=[smem] + [vmem] * 9,
        out_specs=vmem,
        scratch_shapes=[
            pltpu.VMEM((3 * rows, rhs, 2 * rank), F32),
            pltpu.VMEM((2 * devices, rhs, 2 * rank), F32),
            pltpu.VMEM((leaf_dev // 2, rhs, 2 * rank), F32),
            pltpu.VMEM((leaf_dev // 2, rhs, 2 * rank), F32),
            pltpu.VMEM((2, rhs, edge), F32),
            pltpu.SemaphoreType.DMA((2,)),
            pltpu.SemaphoreType.DMA((2,)),
        ],
        compiler_params=pltpu.CompilerParams(
            vmem_limit_bytes=VMEM_BYTES, collective_id=1, has_side_effects=True
        ),
        cost_estimate=pl.CostEstimate(
            flops=2 * 256 * 256 * 256 * 64, bytes_accessed=4 * 2**20, transcendentals=2**21
        ),
        name="downward",
    )(
        far_list.T,
        near,
        leaf_basis,
        transfer,
        table,
        table_left,
        table_right,
        roots,
        transfer_top,
        skeleton_top,
    )


def solution(mesh):
    return jax.shard_map(
        body,
        mesh=mesh,
        in_specs=(
            P(None, "dev"),
            P(None, "dev"),
            P("dev", None, None),
            P("dev", None),
            P("dev", None),
            P("dev", None, None),
            P("dev", None),
            P(),
            P(),
        ),
        out_specs=P(None, "dev"),
        check_vma=False,
    )
```

profile of v0, /device:TPU:13, one launch (start us, length us, event | category | flops | bytes accessed | tf_op | source)
XLA Modules:
  0.0 98.4 jit_solution(17370097598511429458)
XLA Ops:
  0.0 28.2 %upward.1 = (f32[63,8,128]{2,1,0:T(8,128)}, f32[63,8,128]{2,1,0:T(8,128)}, f32[63,8,128]{2,1,0:T(8,128)}, f32[32,8,128]{2,1,0:T(8,128)}, f32[3,16384]{1,0:T(4,12...) custom-call(s32[8,64]{1,0:T(8,128)} %bitcast.4, ...), custom_call_target="tpu_custom_call" | custom-call | flops 2147483648 | bytes 4194304 | tf_op jit(solution)/shard_map/upward/pallas_call | solution.py:635
  28.2 1.6 %slice_convert_fusion = s32[32,1,2]{2,1,0:T(1,128)} fusion(f32[32,8,128]{2,1,0:T(8,128)} %get-tuple-element.15.roots_ref), kind=kLoop, calls=%fused_computation | loop fusion | flops 64 | bytes 512 | tf_op jit(solution)/shard_map/convert_element_type | solution.py:667
  29.8 50.7 %near.1.near_ref = f32[8,32768]{1,0:T(8,128)} custom-call(s32[32,2]{1,0:T(8,128)} %bitcast.3, s32[8,64]{1,0:T(8,128)} %bitcast.5, s32[8,64]{1,0:T(8,128)} %get-tuple-element.16.list_left_ref, s32[8,64]{1,0:T(8,128)} %get-tuple-element.17.list_right_ref, f32[3,16384]{1,0:T(4,128)} %points_ref.3, f32[3,16384]{1,0:T(4,128)} %get-tuple-element.18.points_left_ref, ...), custom_call_target="tpu_custom_call" | custom-call | flops 42949672960 | bytes 2097152 | tf_op jit(solution)/shard_map/near/pallas_call | solution.py:670
  80.5 16.1 %downward.1 = f32[8,16384]{1,0:T(8,128)} custom-call(s32[4,62]{1,0:T(4,128)} %bitcast.6, f32[8,32768]{1,0:T(8,128)} %near.1.near_ref, bf16[64,64,256]{2,1,0:T(8,128)(2,1)} %basis_ref.3, bf16[63,64,128]{2,1,0:T(8,128)(2,1)} %transfer_ref.3, f32[63,8,128]{2,1,0:T(8,128)} %get-tuple-element.22.own_ref, f32[63,8,128]{2,1,0:T(8,128)} %get-tuple-element.23.left_ref, ...), custom_call_target="tpu_custom_call" | custom-call | flops 2147483648 | bytes 4194304 | tf_op jit(solution)/shard_map/downward/pallas_call | solution.py:700
  96.5 1.9 %copy.16 = f32[8,16384]{1,0:T(8,128)} copy(f32[8,16384]{1,0:T(8,128)} %downward.1) | data formatting | bytes 1048576
where the time goes:
time: 99.9 us; the launch traced here: 98.4 us
  Pallas kernels  94.9 us (95%)
  local copies, waits for them, and re-layouts  1.87 us (2%)
  other arithmetic  1.61 us (2%)
    pallas_call x1, Pallas kernels, body(): pl.pallas_call(near_kernel, out_shape=jax.ShapeDtypeStruct((rhs, cells +...  50.7 us
    pallas_call x1, Pallas kernels, body(): pl.pallas_call(up_kernel, out_shape=(table_shape, table_shape, table_shap...  28.2 us
    pallas_call x1, Pallas kernels, body(): pl.pallas_call(down_kernel, out_shape=jax.ShapeDtypeStruct((rhs, cells),...  16.1 us

commit v1 on v0

--- a/solution.py
+++ b/solution.py
@@ -107,8 +107,6 @@
     transfer_ref,
     skeleton_ref,
     table_ref,
-    table_left_ref,
-    table_right_ref,
     roots_ref,
     points_left_ref,
     points_right_ref,
@@ -164,8 +162,6 @@
         beside(vec_ref, vec_right_ref, left, 4),
         beside(list_ref, list_right_ref, left, 5),
     ]
-    table_right = beside(table_ref, table_left_ref, right, 6)
-    table_left = beside(table_ref, table_right_ref, left, 7)
 
     @pl.when(has_right)
     def _():
@@ -223,30 +219,22 @@
         root_copy(shift).wait()
         return carry
 
-    @pl.when(has_right)
-    def _():
-        table_right.start()
-
-    @pl.when(has_left)
-    def _():
-        table_left.start()
-
     lax.fori_loop(1, devices, send_root, 0)
     own_copy = pltpu.make_async_copy(root, mine, own_sem)
     own_copy.start()
 
     @pl.when(has_right)
     def _():
-        for copy in leaf_right + [table_right]:
+        for copy in leaf_right:
             copy.wait_send()
-        for copy in leaf_left + [table_left]:
+        for copy in leaf_left:
             copy.wait_recv()
 
     @pl.when(has_left)
     def _():
-        for copy in leaf_left + [table_left]:
+        for copy in leaf_left:
             copy.wait_send()
-        for copy in leaf_right + [table_right]:
+        for copy in leaf_right:
             copy.wait_recv()
 
     lax.fori_loop(1, devices, wait_root, 0)
@@ -436,8 +424,6 @@
     basis_ref,
     transfer_ref,
     own_ref,
-    left_ref,
-    right_ref,
     roots_ref,
     transfer_top_ref,
     skeleton_top_ref,
@@ -475,29 +461,34 @@
 
     pl.semaphore_wait(barrier, jnp.where(has_right, 1, 0) + jnp.where(has_left, 1, 0))
 
-    def handed_back(start, index, device):
+    def beside(source, arrival, index, device):
         return pltpu.make_async_remote_copy(
-            src_ref=near_ref.at[:, pl.ds(start, edge)],
-            dst_ref=help_ref.at[index],
+            src_ref=source,
+            dst_ref=arrival,
             send_sem=send_sem.at[index],
             recv_sem=recv_sem.at[index],
             device_id=(device,),
             device_id_type=MESH,
         )
 
-    to_right = handed_back(edge + leaf_dev * leaf, 0, right)
-    to_left = handed_back(0, 1, left)
+    upper = near_ref.at[:, pl.ds(edge + leaf_dev * leaf, edge)]
+    lower = near_ref.at[:, pl.ds(0, edge)]
+    to_right = beside(upper, help_ref.at[0], 0, right)
+    to_left = beside(lower, help_ref.at[1], 1, left)
+    table_right = beside(own_ref, wide_ref.at[pl.ds(0, rows)], 2, right)
+    table_left = beside(own_ref, wide_ref.at[pl.ds(2 * rows, rows)], 3, left)
 
     @pl.when(has_right)
     def _():
+        table_right.start()
         to_right.start()
 
     @pl.when(has_left)
     def _():
+        table_left.start()
         to_left.start()
 
-    for part, ref in enumerate((left_ref, own_ref, right_ref)):
-        wide_ref[part * rows : (part + 1) * rows] = ref[...]
+    wide_ref[rows : 2 * rows] = own_ref[...]
     top_ref[0:devices] = roots_ref[...]
 
     def top_row(step, spot):
@@ -518,6 +509,37 @@
             top_ref[top_row(step, spot)] = jnp.concatenate([coef, cells], axis=1)
 
         loop(devices >> step, 16, lift)
+
+    field = None
+    for step in range(top - 1, -1, -1):
+        spot = me >> step
+        mine = top_ref[top_row(step, spot)]
+        sibling = top_ref[top_row(step, spot ^ 1)]
+        coupled = couple(mine[:, rank:], [sibling], [1.0])
+        if field is None:
+            field = coupled
+        else:
+            parent = devices - (devices >> step) + (spot >> 1)
+            both = fold(product(two_pieces(field), transfer_top_ref[parent]))
+            field = jnp.where((spot & 1) == 1, both[:, rank:], both[:, :rank]) + coupled
+
+    @pl.when(has_right)
+    def _():
+        table_right.wait_send()
+        table_left.wait_recv()
+
+    @pl.when(has_left)
+    def _():
+        table_left.wait_send()
+        table_right.wait_recv()
+
+    @pl.when(jnp.logical_not(has_left))
+    def _():
+        wide_ref[0:rows] = jnp.zeros(own_ref.shape, F32)
+
+    @pl.when(jnp.logical_not(has_right))
+    def _():
+        wide_ref[2 * rows : 3 * rows] = jnp.zeros(own_ref.shape, F32)
 
     for level in range(1, local):
         first = level_row(leaf_dev, level)
@@ -540,19 +562,6 @@
 
         loop(count // 2, 4, couple_pair)
 
-    field = None
-    for step in range(top - 1, -1, -1):
-        spot = me >> step
-        mine = top_ref[top_row(step, spot)]
-        sibling = top_ref[top_row(step, spot ^ 1)]
-        coupled = couple(mine[:, rank:], [sibling], [1.0])
-        if field is None:
-            field = coupled
-        else:
-            parent = devices - (devices >> step) + (spot >> 1)
-            both = fold(product(two_pieces(field), transfer_top_ref[parent]))
-            field = jnp.where((spot & 1) == 1, both[:, rank:], both[:, :rank]) + coupled
-
     fields = [field]
     for level in range(local - 1, -1, -1):
         first = level_row(leaf_dev, level + 1)
@@ -623,8 +632,6 @@
     vec_shape = jax.ShapeDtypeStruct(vectors.shape, vectors.dtype)
     (
         table,
-        table_left,
-        table_right,
         roots,
         points_left,
         points_right,
@@ -636,8 +643,6 @@
         up_kernel,
         out_shape=(
             table_shape,
-            table_shape,
-            table_shape,
             jax.ShapeDtypeStruct((devices, rhs, 2 * rank), F32),
             points_shape,
             points_shape,
@@ -647,11 +652,11 @@
             list_shape,
         ),
         in_specs=[vmem] * 6,
-        out_specs=(vmem,) + (hbm,) * 9,
+        out_specs=(vmem,) + (hbm,) * 7,
         scratch_shapes=[
             pltpu.VMEM((leaf_dev // 2, rhs, 2 * rank), F32),
-            pltpu.SemaphoreType.DMA((8,)),
-            pltpu.SemaphoreType.DMA((8,)),
+            pltpu.SemaphoreType.DMA((6,)),
+            pltpu.SemaphoreType.DMA((6,)),
             pltpu.SemaphoreType.DMA((devices,)),
             pltpu.SemaphoreType.DMA((devices,)),
             pltpu.SemaphoreType.DMA,
@@ -700,7 +705,7 @@
     return pl.pallas_call(
         down_kernel,
         out_shape=jax.ShapeDtypeStruct((rhs, cells), F32),
-        in_specs=[smem] + [vmem] * 9,
+        in_specs=[smem] + [vmem] * 7,
         out_specs=vmem,
         scratch_shapes=[
             pltpu.VMEM((3 * rows, rhs, 2 * rank), F32),
@@ -708,8 +713,8 @@
             pltpu.VMEM((leaf_dev // 2, rhs, 2 * rank), F32),
             pltpu.VMEM((leaf_dev // 2, rhs, 2 * rank), F32),
             pltpu.VMEM((2, rhs, edge), F32),
-            pltpu.SemaphoreType.DMA((2,)),
-            pltpu.SemaphoreType.DMA((2,)),
+            pltpu.SemaphoreType.DMA((4,)),
+            pltpu.SemaphoreType.DMA((4,)),
         ],
         compiler_params=pltpu.CompilerParams(
             vmem_limit_bytes=VMEM_BYTES, collective_id=1, has_side_effects=True
@@ -724,8 +729,6 @@
         leaf_basis,
         transfer,
         table,
-        table_left,
-        table_right,
         roots,
         transfer_top,
         skeleton_top,

time: 99.9 us -> 101 us (1.011)
  the two profiles are of different devices: /device:TPU:13 before, /device:TPU:1 now
where the time goes in v1:
time: 101 us; the launch traced here: 100 us
  Pallas kernels  96.8 us (96%)
  local copies, waits for them, and re-layouts  1.87 us (2%)
  other arithmetic  1.61 us (2%)
    pallas_call x1, Pallas kernels, body(): pl.pallas_call(near_kernel, out_shape=jax.ShapeDtypeStruct((rhs, cells +...  52.3 us
    pallas_call x1, Pallas kernels, body(): pl.pallas_call(up_kernel, out_shape=(table_shape, jax.ShapeDtypeStruct((d...  24.4 us
    pallas_call x1, Pallas kernels, body(): pl.pallas_call(down_kernel, out_shape=jax.ShapeDtypeStruct((rhs, cells),...  20.1 us

profile of v1, /device:TPU:1, one launch (start us, length us, event | category | flops | bytes accessed | tf_op | source)
XLA Modules:
  0.0 100.3 jit_solution(5789166831033841257)
XLA Ops:
  0.0 24.4 %upward.1 = (f32[63,8,128]{2,1,0:T(8,128)}, f32[32,8,128]{2,1,0:T(8,128)}, f32[3,16384]{1,0:T(4,128)}, f32[3,16384]{1,0:T(4,128)}, bf16[8,16384]{1,0:T(8,128)(2,...) custom-call(s32[8,64]{1,0:T(8,128)} %bitcast.4, f32[3,16384]{1,0:T(4,128)} %points_ref.3, ...), custom_call_target="tpu_custom_call" | custom-call | flops 2147483648 | bytes 4194304 | tf_op jit(solution)/shard_map/upward/pallas_call | solution.py:642
  24.4 1.6 %slice_convert_fusion = s32[32,1,2]{2,1,0:T(1,128)} fusion(f32[32,8,128]{2,1,0:T(8,128)} %get-tuple-element.13.roots_ref), kind=kLoop, calls=%fused_computation | loop fusion | flops 64 | bytes 512 | tf_op jit(solution)/shard_map/convert_element_type | solution.py:672
  26.0 52.3 %near.1.near_ref = f32[8,32768]{1,0:T(8,128)} custom-call(s32[32,2]{1,0:T(8,128)} %bitcast.3, s32[8,64]{1,0:T(8,128)} %bitcast.5, s32[8,64]{1,0:T(8,128)} %get-tuple-element.14.list_left_ref, s32[8,64]{1,0:T(8,128)} %get-tuple-element.15.list_right_ref, f32[3,16384]{1,0:T(4,128)} %points_ref.3, f32[3,16384]{1,0:T(4,128)} %get-tuple-element.16.points_left_ref, ...), custom_call_target="tpu_custom_call" | custom-call | flops 42949672960 | bytes 2097152 | tf_op jit(solution)/shard_map/near/pallas_call | solution.py:675
  78.4 20.1 %downward.1 = f32[8,16384]{1,0:T(8,128)} custom-call(s32[4,62]{1,0:T(4,128)} %bitcast.6, f32[8,32768]{1,0:T(8,128)} %near.1.near_ref, bf16[64,64,256]{2,1,0:T(8,128)(2,1)} %basis_ref.3, bf16[63,64,128]{2,1,0:T(8,128)(2,1)} %transfer_ref.3, f32[63,8,128]{2,1,0:T(8,128)} %get-tuple-element.20.own_ref, f32[32,8,128]{2,1,0:T(8,128)} %get-tuple-element.13.roots_ref, ...), custom_call_target="tpu_custom_call" | custom-call | flops 2147483648 | bytes 4194304 | tf_op jit(solution)/shard_map/downward/pallas_call | solution.py:705
  98.5 1.9 %copy.16 = f32[8,16384]{1,0:T(8,128)} copy(f32[8,16384]{1,0:T(8,128)} %downward.1) | data formatting | bytes 1048576
